TPU v7x, 32 devices: a whole 2x2x4 slice. The times are simulated.
32 devices in a mesh: slab: 8 (over z, y), rows: 4 (over x, core).
Axes of the slice: x: 2, y: 2, z: 4, core: 2. Of those that a mesh axis runs over, the one named last changes fastest.
Arguments:
- frames: bfloat16 [128, 16, 128, 256], P('slab', 'rows'), may hold values from -6 to 6
- clip_ids: int32 [128], P('slab'), may hold values from 0 to 15, never falling along the last dimension, each value on 1 to 32 neighbouring positions
- norm_gain: float32 [256], replicated, may hold values from 0.1 to 1.9
- norm_shift: float32 [256], replicated, may hold values from -3 to 3
- w_spatial: bfloat16 [3, 3, 256, 256], replicated, may hold values from -0.125 to 0.125
- b_spatial: float32 [256], replicated, may hold values from -3 to 3
- w_time: bfloat16 [3, 256, 256], replicated, may hold values from -0.25 to 0.25
- b_time: float32 [256], replicated, may hold values from -3 to 3
- w_lift: bfloat16 [256, 512], replicated, may hold values from -0.375 to 0.375
- pack_dest: int32 [128], P('slab'), may hold values from 0 to 127, as said below
Outputs:
- packed: bfloat16 [128, 16, 128, 512], P('slab', 'rows')
Inputs may be any that keep to these rules, and one draw needn't show every extreme that they name: `clip_ids`: clip ids never fall and each of the 16 clips has at least one frame. pack_dest is a permutation of the frames; from each aligned block of 16 frames exactly 2 land in each aligned block of 16 positions.
All inputs are finite; a program needn't handle non-finite values.
Results may differ from a plain program's by a relative error of at most 0.0056.
Values may be sent and summed in bfloat16 or wider, within the bound.
A program may use at most 192 MiB of HBM per device.

v0:
```python
import jax
import jax.numpy as jnp
from jax import lax
from jax.sharding import PartitionSpec as P

GROUPS = 32
CLIPS = 16


def padded_2(cells, sides, width):
    for axis, dim in sides:
        count = lax.axis_size(axis)
        ends = count - 1
        head = lax.slice_in_dim(cells, 0, width, axis=dim)
        tail = lax.slice_in_dim(cells, cells.shape[dim] - width, cells.shape[dim], axis=dim)
        cells = jnp.concatenate(
            [
                lax.ppermute(tail, axis, [(i, (i + 1) % count) for i in range(ends)]),
                cells,
                lax.ppermute(head, axis, [((i + 1) % count, i) for i in range(ends)]),
            ],
            axis=dim,
        )
    return cells


def shifted(block, axis, distance):
    devices = range(lax.axis_size(axis))
    route = [(i - distance, i) for i in devices if i - distance in devices]
    return lax.ppermute(block, axis, route)


def route_slots(pack_dest, shards, frame_count):
    per_peer = frame_count // shards
    target = pack_dest // frame_count
    same = target[:, None] == target[None, :]
    earlier = jnp.arange(frame_count)[:, None] < jnp.arange(frame_count)[None, :]
    ranked = jnp.sum(jnp.logical_and(same, earlier).astype(jnp.int32), axis=0)
    slot_of = target * per_peer + ranked
    selector = slot_of[None, :] == jnp.arange(shards * per_peer, dtype=jnp.int32)[:, None]
    position = pack_dest % frame_count
    slot_pos = jnp.sum(selector.astype(jnp.int32) * (position[None, :] + 1), axis=1) - 1
    return (selector.astype(jnp.bfloat16), slot_pos, per_peer)


def place_frames(received, received_pos, frame_count):
    flat = received.reshape((-1,) + received.shape[2:])
    flat_pos = received_pos.reshape(-1)
    placer = (flat_pos[None, :] == jnp.arange(frame_count, dtype=jnp.int32)[:, None]).astype(
        jnp.bfloat16
    )
    return jnp.einsum("tq,qrwd->trwd", placer, flat, preferred_element_type=jnp.float32).astype(
        jnp.bfloat16
    )


def body(
    frames, clip_ids, norm_gain, norm_shift, w_spatial, b_spatial, w_time, b_time, w_lift, pack_dest
):
    frame_count, band, width, chan = frames.shape
    per_group = chan // GROUPS
    shards = lax.axis_size("slab")
    onehot = (clip_ids[:, None] == jnp.arange(CLIPS, dtype=jnp.int32)[None, :]).astype(jnp.float32)
    grouped = frames.reshape(frame_count, band * width, GROUPS, per_group)
    sums = jnp.sum(grouped, axis=(1, 3), dtype=jnp.float32)
    squares = jnp.sum(jnp.square(grouped.astype(jnp.float32)), axis=(1, 3))
    local_counts = jnp.sum(onehot, axis=0) * (band * width * per_group)
    clip_sum, clip_sq, counts = lax.psum(
        (
            jnp.dot(onehot.T, sums, precision=lax.Precision.HIGHEST),
            jnp.dot(onehot.T, squares, precision=lax.Precision.HIGHEST),
            local_counts,
        ),
        ("slab", "rows"),
    )
    mean = clip_sum / counts[:, None]
    var = clip_sq / counts[:, None] - mean * mean
    rstd = 1.0 / jnp.sqrt(var + 1e-05)
    frame_mean = jnp.dot(onehot, mean, precision=lax.Precision.HIGHEST)
    frame_rstd = jnp.dot(onehot, rstd, precision=lax.Precision.HIGHEST)
    normed = (grouped.astype(jnp.float32) - frame_mean[:, None, :, None]) * frame_rstd[
        :, None, :, None
    ]
    normed = normed.reshape(frame_count, band, width, chan)
    normed = jax.nn.silu(normed * norm_gain + norm_shift).astype(jnp.bfloat16)
    padded = padded_2(normed, (("rows", 1),), 1)
    padded = jnp.pad(padded, ((0, 0), (0, 0), (1, 1), (0, 0)))
    total = jnp.zeros((frame_count, band, width, chan), jnp.float32) + b_spatial
    for a in range(3):
        for b in range(3):
            total = total + jnp.einsum(
                "trwc,cd->trwd",
                padded[:, a : a + band, b : b + width],
                w_spatial[a, b],
                preferred_element_type=jnp.float32,
            )
    spatial = total.astype(jnp.bfloat16)
    prior_frames, prior_ids = shifted((spatial[-2:], clip_ids[-2:]), "slab", 1)
    extended = jnp.concatenate([prior_frames, spatial], axis=0)
    extended_ids = jnp.concatenate([prior_ids, clip_ids], axis=0)
    accum = frames.astype(jnp.float32) + b_time
    for k in range(3):
        same = (extended_ids[2 - k : 2 - k + frame_count] == clip_ids).astype(jnp.float32)
        term = jnp.einsum(
            "trwc,cd->trwd",
            extended[2 - k : 2 - k + frame_count],
            w_time[k],
            preferred_element_type=jnp.float32,
        )
        accum = accum + same[:, None, None, None] * term
    lifted_in = accum.astype(jnp.bfloat16)
    selector, slot_pos, per_peer = route_slots(pack_dest, shards, frame_count)
    outgoing = jnp.einsum(
        "qt,trwd->qrwd", selector, lifted_in, preferred_element_type=jnp.float32
    ).astype(jnp.bfloat16)
    outgoing = outgoing.reshape((shards, per_peer) + outgoing.shape[1:])
    received, received_pos = (
        lax.all_to_all(outgoing, "slab", split_axis=0, concat_axis=0, tiled=True),
        lax.all_to_all(
            slot_pos.reshape(shards, per_peer), "slab", split_axis=0, concat_axis=0, tiled=True
        ),
    )
    placed = place_frames(received, received_pos, frame_count)
    packed = jnp.einsum("trwc,cd->trwd", placed, w_lift, preferred_element_type=jnp.float32).astype(
        jnp.bfloat16
    )
    return packed


def solution(mesh):
    in_specs = (
        P("slab", "rows", None, None),
        P("slab"),
        P(),
        P(),
        P(),
        P(),
        P(),
        P(),
        P(),
        P("slab"),
    )
    out_specs = P("slab", "rows", None, None)
    return jax.shard_map(body, mesh=mesh, in_specs=in_specs, out_specs=out_specs, check_vma=False)
```

profile of v0, /device:TPU:0, one launch (start us, length us, event | category | flops | bytes accessed | tf_op | source)
XLA Modules:
  0.0 310.6 jit_solution(7632435565143498229)
XLA Ops:
  0.0 3.4 %convert_reduce_fusion = (f32[16,256]{1,0:T(8,128)S(1)}, f32[16,256]{1,0:T(8,128)S(1)}) fusion(bf16[16,4,128,256]{3,2,1,0:T(8,128)(2,1)} %param.10), kind=kLoop, calls=%fused_computation.4 | loop fusion | flops 8380416 | bytes 4227072 | tf_op jit(solution)/shard_map/reduce_sum | solution.py:65
  3.4 0.1 copy.32
  3.5 0.7 convert_reduce_fusion.1
  4.3 0.9 fusion.89
  5.2 0.1 copy.29
  5.3 0.9 fusion.91
  6.2 42.2 %all-reduce.1 = (f32[16,32]{1,0:T(8,128)S(1)}, f32[16]{0:T(128)S(1)}, f32[16,32]{1,0:T(8,128)S(1)}) all-reduce(f32[16,32]{1,0:T(8,128)S(1)} %fusion.89, f32[16]{0:T(128)S(1)} %broadcast_multiply_fusion, f32[16,32]{1,0:T(8,128)S(1)} %fusion.91), channel_id=1, replica_groups=mesh['slab'=8,'rows'=4] {'slab','rows'}, use_global_device_ids=true, to_apply=%region_9.10 | all-reduce | flops 1040 | bytes 8320 | tf_op jit(solution)/shard_map/psum | solution.py:68
  48.5 0.9 fusion.82
  49.4 1.0 fusion.76
  50.6 4.7 %fusion.13 = bf16[16,4,128,256]{3,2,1,0:T(8,128)(2,1)S(1)} fusion(bf16[16,4,128,256]{3,2,1,0:T(8,128)(2,1)} %param.10, f32[256]{0:T(256)} %param.13, f32[256]{0:T(256)} %param.12, f32[16,256]{1,0:T(8,128)S(1)} %copy.34, f32[16,256]{1,0:T(8,128)S(1)} %copy.31), kind=kLoop, calls=%fused_computation.19 | loop fusion | flops 20971520 | bytes 8423424 | tf_op jit(solution)/shard_map/convert_element_type | solution.py:85
  55.3 2.0 copy-done.1
  57.3 1.5 fusion.107
  58.9 1.3 collective-permute-start
  60.2 1.3 collective-permute-start.1
  61.5 0.6 slice.110
  62.2 4.2 %collective-permute-start.2 = (s32[2]{0:T(128)}, s32[2]{0:T(128)S(1)}, u32[]{:S(2)}, u32[]{:S(2)}) collective-permute-start(s32[2]{0:T(128)} %slice.110), channel_id=1, source_target_pairs={{0,4},{4,8},{8,12},{12,16},{16,20},{20,24},{24,28},{1,5},{5,9},{9,... | collective-permute-start | bytes 32 | tf_op jit(solution)/shard_map/ppermute | solution.py:30
  66.4 0.1 convert_reduce_fusion.2
  66.5 0.1 select_reduce_fusion
  66.6 0.7 sub.27
  67.3 3.6 %all-to-all-start = ((s32[8,1,2]{2,1,0:T(1,128)}), s32[8,1,2]{2,1,0:T(1,128)S(1)}, u32[]{:S(2)}, u32[]{:S(2)}) async-start(s32[8,1,2]{2,1,0:T(1,128)} %bitcast), calls=%async_computation | async-start | bytes 8192 | tf_op jit(solution)/shard_map/all_to_all | solution.py:119
  70.9 6.8 %fusion.58 = f32[16,4,128,256]{3,2,1,0:T(8,128)} fusion(bf16[16,4,128,256]{3,2,1,0:T(8,128)(2,1)} %copy-done.1, bf16[3,3,256,256]{3,2,1,0:T(8,128)(2,1)S(1)} %copy-done.4), kind=kOutput, calls=%fused_computation.64 | convolution fusion | flops 1073741824 | bytes 12713984 | tf_op jit(solution)/shard_map/trwc,cd->trwd/dot_general | solution.py:91
  77.7 0.1 pad_add_fusion
  77.9 3.5 %fusion.19 = bf16[16,6,130,256]{3,2,1,0:T(8,128)(2,1)S(1)} fusion(bf16[16,1,128,256]{3,2,1,0:T(8,128)(2,1)S(1)} %collective-permute-done.1, bf16[16,4,128,256]{3,2,1,0:T(8,128)(2,1)S(1)} %copy-done.2, bf16[16,1,128,256]{3,2,1,0:T(8,128)(2,1)S(1)} %collective-permute-done), kind=kLoop, calls=%fused_computation.27 | loop fusion | flops 38338560 | bytes 12681216 | tf_op jit(solution)/shard_map/concatenate | solution.py:16
  81.4 4.5 %fusion.30 = f32[16,4,128,256]{3,2,1,0:T(8,128)} fusion(bf16[16,6,130,256]{3,2,1,0:T(8,128)(2,1)S(1)} %fusion.19, bf16[3,3,256,256]{3,2,1,0:T(8,128)(2,1)S(1)} %copy-done.4), kind=kOutput, calls=%fused_computation.39 | convolution fusion | flops 1073741824 | bytes 12713984 | tf_op jit(solution)/shard_map/trwc,cd->trwd/dot_general | solution.py:91
  85.8 4.5 %fusion.32 = f32[16,4,128,256]{3,2,1,0:T(8,128)} fusion(bf16[16,6,130,256]{3,2,1,0:T(8,128)(2,1)S(1)} %fusion.19, bf16[3,3,256,256]{3,2,1,0:T(8,128)(2,1)S(1)} %copy-done.4), kind=kOutput, calls=%fused_computation.41 | convolution fusion | flops 1073741824 | bytes 12713984 | tf_op jit(solution)/shard_map/trwc,cd->trwd/dot_general | solution.py:91
  90.3 4.5 %fusion.34 = f32[16,4,128,256]{3,2,1,0:T(8,128)} fusion(bf16[16,6,130,256]{3,2,1,0:T(8,128)(2,1)S(1)} %fusion.19, bf16[3,3,256,256]{3,2,1,0:T(8,128)(2,1)S(1)} %copy-done.4), kind=kOutput, calls=%fused_computation.43 | convolution fusion | flops 1073741824 | bytes 12713984 | tf_op jit(solution)/shard_map/trwc,cd->trwd/dot_general | solution.py:91
  94.8 4.5 %fusion.36 = f32[16,4,128,256]{3,2,1,0:T(8,128)} fusion(bf16[16,6,130,256]{3,2,1,0:T(8,128)(2,1)S(1)} %fusion.19, bf16[3,3,256,256]{3,2,1,0:T(8,128)(2,1)S(1)} %copy-done.4), kind=kOutput, calls=%fused_computation.45 | convolution fusion | flops 1073741824 | bytes 12713984 | tf_op jit(solution)/shard_map/trwc,cd->trwd/dot_general | solution.py:91
  99.3 4.5 %fusion.38 = f32[16,4,128,256]{3,2,1,0:T(8,128)} fusion(bf16[16,6,130,256]{3,2,1,0:T(8,128)(2,1)S(1)} %fusion.19, bf16[3,3,256,256]{3,2,1,0:T(8,128)(2,1)S(1)} %copy-done.4), kind=kOutput, calls=%fused_computation.47 | convolution fusion | flops 1073741824 | bytes 12713984 | tf_op jit(solution)/shard_map/trwc,cd->trwd/dot_general | solution.py:91
  103.7 4.4 %fusion.20 = f32[16,4,128,256]{3,2,1,0:T(8,128)} fusion(bf16[16,4,128,256]{3,2,1,0:T(8,128)(2,1)S(1)} %copy-done.2, bf16[16,1,128,256]{3,2,1,0:T(8,128)(2,1)S(1)} %collective-permute-done, bf16[3,3,256,256]{3,2,1,0:T(8,128)(2,1)S(1)} %copy-done.4), kind=kOutput, calls=%fused_computation.28 | convolution fusion | flops 1084227584 | bytes 13762560 | tf_op jit(solution)/shard_map/trwc,cd->trwd/dot_general | solution.py:91
  108.2 4.6 %fusion.24 = f32[16,4,128,256]{3,2,1,0:T(8,128)} fusion(bf16[16,1,128,256]{3,2,1,0:T(8,128)(2,1)S(1)} %collective-permute-done.1, bf16[16,4,128,256]{3,2,1,0:T(8,128)(2,1)S(1)} %copy-done.2, bf16[3,3,256,256]{3,2,1,0:T(8,128)(2,1)S(1)} %copy-done.4), kind=kOutput, calls=%fused_computation.32 | convolution fusion | flops 1084227584 | bytes 13762560 | tf_op jit(solution)/shard_map/trwc,cd->trwd/dot_general | solution.py:91
  112.8 21.5 %add_convert_fusion = bf16[16,4,128,256]{3,2,1,0:T(8,128)(2,1)S(1)} fusion(f32[16,4,128,256]{3,2,1,0:T(8,128)} %fusion.24, f32[16,4,128,256]{3,2,1,0:T(8,128)} %fusion.30, f32[16,4,128,256]{3,2,1,0:T(8,128)} %fusion.32, f32[16,4,128,256]{3,2,1,0:T(8,128)} %fusion.58, f32[16,4,128,256]{3,2,1,0:T(8,128)} %fusion.34, f32[16,4,128,256]{3,2,1,0:T(8,128)} %fusion.36, ...), kind=kOutput, calls=%fused_computation.21 | convolution fusion | flops 1094713344 | bytes 75629568 | tf_op jit(solution)/shard_map/trwc,cd->trwd/dot_general | solution.py:91
  134.4 4.2 %collective-permute-start.3 = (bf16[2,4,128,256]{3,2,1,0:T(8,128)(2,1)S(1)}, bf16[2,4,128,256]{3,2,1,0:T(8,128)(2,1)S(1)}, u32[]{:S(2)}, u32[]{:S(2)}) collective-permute-start(bf16[2,4,128,256]{3,2,1,0:T(8,128)(2,1)S(1)} %slice.126), channel_id=1, source_target_pairs={{0,4},{4,8},{8,12},{12,16},{16,20},{20,24},{24,28},{1,5},{5,9},{9,... | collective-permute-start | bytes 1572872 | tf_op jit(solution)/shard_map/ppermute | solution.py:30
  138.6 4.7 %fusion.52 = f32[16,4,128,256]{3,2,1,0:T(8,128)} fusion(bf16[16,4,128,256]{3,2,1,0:T(8,128)(2,1)S(1)} %add_convert_fusion, bf16[3,256,256]{2,1,0:T(8,128)(2,1)S(1)} %copy-done.5), kind=kOutput, calls=%fused_computation.58 | convolution fusion | flops 1073741824 | bytes 12713984 | tf_op jit(solution)/shard_map/trwc,cd->trwd/dot_general | solution.py:104
  143.3 6.4 %collective-permute-done.3 = bf16[2,4,128,256]{3,2,1,0:T(8,128)(2,1)S(1)} collective-permute-done((bf16[2,4,128,256]{3,2,1,0:T(8,128)(2,1)S(1)}, bf16[2,4,128,256]{3,2,1,0:T(8,128)(2,1)S(1)}, u32[]{:S(2)}, u32[]{:S(2)}) %collective-permute-start.3) | collective-permute-done | bytes 524320 | tf_op jit(solution)/shard_map/ppermute | solution.py:30
  149.7 4.5 %fusion.45 = f32[16,4,128,256]{3,2,1,0:T(8,128)} fusion(bf16[16,4,128,256]{3,2,1,0:T(8,128)(2,1)S(1)} %add_convert_fusion, bf16[2,4,128,256]{3,2,1,0:T(8,128)(2,1)S(1)} %collective-permute-done.3, bf16[3,256,256]{2,1,0:T(8,128)(2,1)S(1)} %copy-done.5), kind=kOutput, calls=%fused_computation.52 | convolution fusion | flops 1083179008 | bytes 13238272 | tf_op jit(solution)/shard_map/trwc,cd->trwd/dot_general | solution.py:104
  154.2 8.7 %fusion.4 = bf16[16,4,128,256]{3,2,1,0:T(8,128)(2,1)} fusion(f32[16,4,128,256]{3,2,1,0:T(8,128)} %fusion.52, bf16[16,4,128,256]{3,2,1,0:T(8,128)(2,1)S(1)} %copy-done.3, f32[16,4,128,256]{3,2,1,0:T(8,128)} %fusion.45, f32[16]{0:T(128)S(1)} %get-tuple-element.13, f32[16]{0:T(128)S(1)} %get-tuple-element.12, f32[256]{0:T(256)S(1)} %copy-done.7, ...), kind=kOutput, calls=%fused_computation.10 | convolution fusion | flops 1099956224 | bytes 30017536 | tf_op jit(solution)/shard_map/trwc,cd->trwd/dot_general | solution.py:104
  162.9 6.7 %fusion.46 = bf16[16,4,128,256]{3,0,2,1:T(8,128)(2,1)} fusion(bf16[16,4,128,256]{3,2,1,0:T(8,128)(2,1)} %fusion.4, s32[16]{0:T(128)S(1)} %multiply_add_fusion), kind=kOutput, calls=%fused_computation.53 | convolution fusion | flops 69206272 | bytes 8388672 | tf_op jit(solution)/shard_map/qt,trwd->qrwd/dot_general | solution.py:113
  169.6 7.2 %reshape.45 = bf16[8,2,4,128,256]{4,1,0,3,2:T(2,128)(2,1)} reshape(bf16[16,4,128,256]{3,0,2,1:T(8,128)(2,1)} %fusion.46) | data formatting | bytes 8388608 | tf_op jit(solution)/shard_map/reshape | solution.py:116
  176.8 8.6 %copy.36 = bf16[8,2,4,128,256]{4,1,3,2,0:T(2,128)(2,1)} copy(bf16[8,2,4,128,256]{4,1,0,3,2:T(2,128)(2,1)} %reshape.45) | data formatting | bytes 8388608 | tf_op jit(solution)/shard_map/reshape | solution.py:116
  185.4 6.5 %all-to-all-start.1 = ((bf16[8,2,4,128,256]{4,1,3,2,0:T(2,128)(2,1)}), bf16[8,2,4,128,256]{4,1,3,2,0:T(2,128)(2,1)}, u32[]{:S(2)}, u32[]{:S(2)}) async-start(bf16[8,2,4,128,256]{4,1,3,2,0:T(2,128)(2,1)} %copy.36), calls=%async_computation.1 | async-start | bytes 8388608 | tf_op jit(solution)/shard_map/all_to_all | solution.py:118
  191.9 0.5 broadcast.99
  192.4 0.6 reduce.7
  193.1 0.1 eq.31
  193.1 93.2 %all-to-all-done.1 = bf16[8,2,4,128,256]{4,1,3,2,0:T(2,128)(2,1)} async-done(((bf16[8,2,4,128,256]{4,1,3,2,0:T(2,128)(2,1)}), bf16[8,2,4,128,256]{4,1,3,2,0:T(2,128)(2,1)}, u32[]{:S(2)}, u32[]{:S(2)}) %all-to-all-start.1) | async-done | bytes 4194336 | tf_op jit(solution)/shard_map/all_to_all | solution.py:118
  286.4 7.4 %copy.37 = bf16[8,2,4,128,256]{4,1,0,3,2:T(2,128)(2,1)} copy(bf16[8,2,4,128,256]{4,1,3,2,0:T(2,128)(2,1)} %all-to-all-done.1) | data formatting | bytes 8388608 | tf_op jit(solution)/shard_map/all_to_all | solution.py:118
  293.7 7.2 %reshape.46 = bf16[16,4,128,256]{3,0,2,1:T(8,128)(2,1)} reshape(bf16[8,2,4,128,256]{4,1,0,3,2:T(2,128)(2,1)} %copy.37) | data formatting | bytes 8388608 | tf_op jit(solution)/shard_map/reshape | solution.py:47
  300.9 3.4 %convolution_convert_fusion.1 = bf16[16,4,128,256]{3,0,2,1:T(8,128)(2,1)S(1)} fusion(bf16[16,4,128,256]{3,0,2,1:T(8,128)(2,1)} %reshape.46, s32[16]{0:T(128)S(1)} %eq.31), kind=kOutput, calls=%fused_computation.54 | convolution fusion | flops 69206272 | bytes 8388672 | tf_op jit(solution)/shard_map/tq,qrwd->trwd/dot_general | solution.py:52
  304.4 6.3 %convolution_convert_fusion = bf16[16,4,128,512]{3,2,1,0:T(8,128)(2,1)} fusion(bf16[16,4,128,256]{3,0,2,1:T(8,128)(2,1)S(1)} %convolution_convert_fusion.1, bf16[256,512]{1,0:T(8,128)(2,1)S(1)} %copy-done), kind=kOutput, calls=%fused_computation.25 | convolution fusion | flops 2151677952 | bytes 12845056 | tf_op jit(solution)/shard_map/trwc,cd->trwd/dot_general | solution.py:124
  (37 shorter events, 0.4 us)
Async XLA Ops:
  0.0 304.4 %copy-start = (bf16[256,512]{1,0:T(8,128)(2,1)S(1)}, bf16[256,512]{1,0:T(8,128)(2,1)}, u32[]{:S(2)}) copy-start(bf16[256,512]{1,0:T(8,128)(2,1)} %param.18) | copy-start | bytes 786436
  49.4 12.1 %copy-start.8 = (s32[16]{0:T(128)S(1)}, s32[16]{0:T(128)}, u32[]{:S(2)}) copy-start(s32[16]{0:T(128)} %param.11) | copy-start | bytes 196
  49.4 17.0 %copy-start.10 = (s32[16]{0:T(128)S(1)}, s32[16]{0:T(128)}, u32[]{:S(2)}) copy-start(s32[16]{0:T(128)} %param.19) | copy-start | bytes 196
  49.4 21.5 %copy-start.4 = (bf16[3,3,256,256]{3,2,1,0:T(8,128)(2,1)S(1)}, bf16[3,3,256,256]{3,2,1,0:T(8,128)(2,1)}, u32[]{:S(2)}) copy-start(bf16[3,3,256,256]{3,2,1,0:T(8,128)(2,1)} %param.14) | copy-start | bytes 3538948
  55.3 2.0 copy-start.1
  58.9 19.0 %collective-permute-start = (bf16[16,1,128,256]{3,2,1,0:T(8,128)(2,1)}, bf16[16,1,128,256]{3,2,1,0:T(8,128)(2,1)S(1)}, u32[]{:S(2)}, u32[]{:S(2)}) collective-permute-start(bf16[16,1,128,256]{3,2,1,0:T(8,128)(2,1)} %get-tuple-element.10), channel_id=1, source_target_pairs={{0,1},{1,2},{2,3},{4,5},{5,6},{6,7},{8,9},{9,10},{10,11},{12,13},{... | collective-permute-start | bytes 3145736 | tf_op jit(solution)/shard_map/ppermute | solution.py:18
  60.2 17.7 %collective-permute-start.1 = (bf16[16,1,128,256]{3,2,1,0:T(8,128)(2,1)}, bf16[16,1,128,256]{3,2,1,0:T(8,128)(2,1)S(1)}, u32[]{:S(2)}, u32[]{:S(2)}) collective-permute-start(bf16[16,1,128,256]{3,2,1,0:T(8,128)(2,1)} %get-tuple-element.11), channel_id=1, source_target_pairs={{1,0},{2,1},{3,2},{5,4},{6,5},{7,6},{9,8},{10,9},{11,10},{13,12},{... | collective-permute-start | bytes 3145736 | tf_op jit(solution)/shard_map/ppermute | solution.py:20
  62.2 15.6 %collective-permute-start.2 = (s32[2]{0:T(128)}, s32[2]{0:T(128)S(1)}, u32[]{:S(2)}, u32[]{:S(2)}) collective-permute-start(s32[2]{0:T(128)} %slice.110), channel_id=1, source_target_pairs={{0,4},{4,8},{8,12},{12,16},{16,20},{20,24},{24,28},{1,5},{5,9},{9,... | collective-permute-start | bytes 32 | tf_op jit(solution)/shard_map/ppermute | solution.py:30
  67.3 118.1 %all-to-all-start = ((s32[8,1,2]{2,1,0:T(1,128)}), s32[8,1,2]{2,1,0:T(1,128)S(1)}, u32[]{:S(2)}, u32[]{:S(2)}) async-start(s32[8,1,2]{2,1,0:T(1,128)} %bitcast), calls=%async_computation | async-start | bytes 8192 | tf_op jit(solution)/shard_map/all_to_all | solution.py:119
  70.9 6.9 %copy-start.9 = (s32[16]{0:T(128)S(1)}, s32[16]{0:T(128)}, u32[]{:S(2)}) copy-start(s32[16]{0:T(128)} %param.11) | copy-start | bytes 196
  70.9 7.0 %copy-start.2 = (bf16[16,4,128,256]{3,2,1,0:T(8,128)(2,1)S(1)}, bf16[16,4,128,256]{3,2,1,0:T(8,128)(2,1)}, u32[]{:S(2)}) copy-start(bf16[16,4,128,256]{3,2,1,0:T(8,128)(2,1)} %copy-done.1) | copy-start | bytes 12582916
  108.2 4.6 %copy-start.6 = (f32[256]{0:T(256)S(1)}, f32[256]{0:T(256)}, u32[]{:S(2)}) copy-start(f32[256]{0:T(256)} %param.15) | copy-start | bytes 3076
  112.8 25.8 %copy-start.5 = (bf16[3,256,256]{2,1,0:T(8,128)(2,1)S(1)}, bf16[3,256,256]{2,1,0:T(8,128)(2,1)}, u32[]{:S(2)}) copy-start(bf16[3,256,256]{2,1,0:T(8,128)(2,1)} %param.16) | copy-start | bytes 1179652
  134.4 15.3 %collective-permute-start.3 = (bf16[2,4,128,256]{3,2,1,0:T(8,128)(2,1)S(1)}, bf16[2,4,128,256]{3,2,1,0:T(8,128)(2,1)S(1)}, u32[]{:S(2)}, u32[]{:S(2)}) collective-permute-start(bf16[2,4,128,256]{3,2,1,0:T(8,128)(2,1)S(1)} %slice.126), channel_id=1, source_target_pairs={{0,4},{4,8},{8,12},{12,16},{16,20},{20,24},{24,28},{1,5},{5,9},{9,... | collective-permute-start | bytes 1572872 | tf_op jit(solution)/shard_map/ppermute | solution.py:30
  143.3 10.9 %copy-start.3 = (bf16[16,4,128,256]{3,2,1,0:T(8,128)(2,1)S(1)}, bf16[16,4,128,256]{3,2,1,0:T(8,128)(2,1)}, u32[]{:S(2)}) copy-start(bf16[16,4,128,256]{3,2,1,0:T(8,128)(2,1)} %param.10) | copy-start | bytes 12582916
  143.3 10.9 %copy-start.7 = (f32[256]{0:T(256)S(1)}, f32[256]{0:T(256)}, u32[]{:S(2)}) copy-start(f32[256]{0:T(256)} %param.17) | copy-start | bytes 3076
  185.4 101.0 %all-to-all-start.1 = ((bf16[8,2,4,128,256]{4,1,3,2,0:T(2,128)(2,1)}), bf16[8,2,4,128,256]{4,1,3,2,0:T(2,128)(2,1)}, u32[]{:S(2)}, u32[]{:S(2)}) async-start(bf16[8,2,4,128,256]{4,1,3,2,0:T(2,128)(2,1)} %copy.36), calls=%async_computation.1 | async-start | bytes 8388608 | tf_op jit(solution)/shard_map/all_to_all | solution.py:118
where the time goes:
time: 311 us
  waiting for transfers between devices  99.7 us (32%)
  matrix products  97.8 us (31%)
  blocking collectives  42.2 us (14%)
  local copies, waits for them, and re-layouts  36.2 us (12%)
  starting transfers between devices  21.1 us (7%)
  other arithmetic  13.3 us (4%)
    all_to_all x1, waiting for transfers between devices, body(): lax.all_to_all(outgoing, 'slab', split_axis=0, concat_axis=0, tiled=True)  93.2 us
    dot_general x9, matrix products, body(): jnp.einsum('trwc,cd->trwd', padded[:, a:a + band, b:b + width], w_spatial...  59.8 us
    psum x1, blocking collectives, body(): lax.psum((jnp.dot(onehot.T, sums, precision=lax.Precision.HIGHEST), jnp.d...  42.2 us
    dot_general x3, matrix products, body(): jnp.einsum('trwc,cd->trwd', extended[2 - k:2 - k + frame_count], w_time[k...  17.8 us
    reshape x2, local copies, waits for them, and re-layouts, body(): outgoing = outgoing.reshape((shards, per_peer) + outgoing.shape[1:])  15.8 us
    ppermute x2, starting transfers between devices, shifted(): return lax.ppermute(block, axis, route)  8.35 us
    all_to_all x1, local copies, waits for them, and re-layouts, body(): lax.all_to_all(outgoing, 'slab', split_axis=0, concat_axis=0, tiled=True)  7.35 us
    reshape x1, local copies, waits for them, and re-layouts, place_frames(): flat = received.reshape((-1,) + received.shape[2:])  7.21 us
  transfers between devices with their start and end apart: 6, of which 2 were waited for; matrix products, arithmetic and copies ran while one was open for 34% of the time, Pallas kernels for 0%

commit v1 on v0

v1 whole, which is shorter than its diff:
```python
import functools

import jax
import jax.numpy as jnp
from jax import lax
from jax.experimental import pallas as pl
from jax.experimental.pallas import tpu as pltpu
from jax.sharding import PartitionSpec as P

GROUPS = 32
CLIPS = 16
BACK = 2
LEAD = 8
DIRECT = 4
MESH = pl.DeviceIdType.MESH
HIGH = lax.Precision.HIGHEST
F32 = jnp.float32
BF16 = jnp.bfloat16


def flipped(index, mask, count):
    out, bit = 0, 1
    while bit < count:
        out = out + lax.rem(lax.rem(index // bit, 2) + lax.rem(mask // bit, 2), 2) * bit
        bit *= 2
    return out


def block_kernel(
    shards,
    bands,
    width,
    order_ref,
    frames_ref,
    ids_ref,
    pos_ref,
    gain_ref,
    shift_ref,
    wsp_ref,
    bsp_ref,
    wtm_ref,
    btm_ref,
    got_ref,
    gotpos_ref,
    xin,
    idtab,
    mean_t,
    scale_t,
    nbuf,
    spat,
    sendbuf,
    rbuf,
    sbuf,
    load_sem,
    halo_send,
    halo_recv,
    r_send,
    r_recv,
    s_send,
    s_recv,
    p_send,
    p_recv,
    x_send,
    x_recv,
    own_sem,
):
    count, cells, chan = frames_ref.shape
    per_peer = count // shards
    per_group = chan // GROUPS
    band = cells // width
    me = lax.axis_index("slab")
    row = lax.axis_index("rows")
    direct = min(DIRECT, (shards - 1) * per_peer)

    def load(t):
        return pltpu.make_async_copy(
            frames_ref.at[t], xin.at[t + BACK, pl.ds(width, cells)], load_sem.at[t]
        )

    @pl.loop(0, count)
    def _(t):
        load(t).start()

    barrier = pltpu.get_barrier_semaphore()
    for o in range(1, bands):
        pl.semaphore_signal(
            barrier, inc=1, device_id=(me, lax.rem(row + o, bands)), device_id_type=MESH
        )
    for o in range(1, shards):
        pl.semaphore_signal(
            barrier, inc=1, device_id=(lax.rem(me + o, shards), row), device_id_type=MESH
        )
    for a in (1, shards - 1):
        for b in (1, bands - 1):
            pl.semaphore_signal(
                barrier,
                inc=1,
                device_id=(lax.rem(me + a, shards), lax.rem(row + b, bands)),
                device_id_type=MESH,
            )
    pl.semaphore_wait(barrier, bands - 1 + shards - 1 + 4)

    top = pl.ds(0, width)
    bottom = pl.ds(width + cells, width)
    first = pl.ds(0, width)
    last = pl.ds(cells - width, width)
    own = pl.ds(BACK, count)
    tail = pl.ds(count - BACK, BACK)
    prior = pl.ds(0, BACK)
    up_slab = lax.rem(me + 1, shards)
    up_row = lax.rem(row + 1, bands)
    down_row = lax.rem(row + bands - 1, bands)

    def halo(i, src, dst, slab, band_index):
        return pltpu.make_async_remote_copy(
            src_ref=src,
            dst_ref=dst,
            send_sem=halo_send.at[i],
            recv_sem=halo_recv.at[i],
            device_id=(slab, band_index),
            device_id_type=MESH,
        )

    halos = (
        (
            halo(0, frames_ref.at[tail], xin.at[prior, pl.ds(width, cells)], up_slab, row),
            me < shards - 1,
            me > 0,
        ),
        (
            halo(1, frames_ref.at[tail, last], xin.at[prior, top], up_slab, up_row),
            jnp.logical_and(me < shards - 1, row < bands - 1),
            jnp.logical_and(me > 0, row > 0),
        ),
        (
            halo(2, frames_ref.at[tail, first], xin.at[prior, bottom], up_slab, down_row),
            jnp.logical_and(me < shards - 1, row > 0),
            jnp.logical_and(me > 0, row < bands - 1),
        ),
        (
            halo(3, frames_ref.at[:, last], xin.at[own, top], me, up_row),
            row < bands - 1,
            row > 0,
        ),
        (
            halo(4, frames_ref.at[:, first], xin.at[own, bottom], me, down_row),
            row > 0,
            row < bands - 1,
        ),
        (
            halo(5, ids_ref.at[pl.ds(count - LEAD, LEAD)], idtab.at[pl.ds(0, LEAD)], up_slab, row),
            me < shards - 1,
            me > 0,
        ),
    )
    for copy, sends, _ in halos:

        @pl.when(sends)
        def _(copy=copy):
            copy.start()

    def place(d):
        return pltpu.make_async_remote_copy(
            src_ref=pos_ref.at[d],
            dst_ref=gotpos_ref.at[me],
            send_sem=p_send.at[d],
            recv_sem=p_recv.at[me],
            device_id=(d, row),
            device_id_type=MESH,
        )

    idtab[pl.ds(LEAD, count), :] = ids_ref[...]
    clip_row = lax.broadcasted_iota(jnp.int32, (CLIPS, chan), 0)
    zero = jnp.zeros((CLIPS, chan), F32)

    def stats(t, carry):
        total, squares, number = carry
        load(t).wait()
        x = xin[t + BACK, pl.ds(width, cells), :].astype(F32)
        one = jnp.sum(x, axis=0, keepdims=True)
        two = jnp.sum(x * x, axis=0, keepdims=True)
        mine = clip_row == ids_ref[pl.ds(t, 1), :]
        return (
            total + jnp.where(mine, one, 0.0),
            squares + jnp.where(mine, two, 0.0),
            number + jnp.where(mine, 1.0, 0.0),
        )

    total, squares, number = lax.fori_loop(0, count, stats, (zero, zero, zero))
    lanes = 128
    channel = lax.broadcasted_iota(jnp.int32, (chan, lanes), 0)
    lane = lax.broadcasted_iota(jnp.int32, (chan, lanes), 1)

    def member(channel, lane, start):
        low = (lane - start) * per_group
        return jnp.logical_and(channel >= low, channel < low + per_group).astype(F32)

    table = jnp.dot(
        total, member(channel, lane, 0), precision=HIGH, preferred_element_type=F32
    ) + jnp.dot(
        squares, member(channel, lane, GROUPS), precision=HIGH, preferred_element_type=F32
    )
    lane_c = lax.broadcasted_iota(jnp.int32, (CLIPS, lanes), 1)
    table = jnp.where(lane_c == 2 * GROUPS, number[:, :lanes] * float(cells * per_group), table)

    rbuf[row] = table

    def across_rows(peer, src):
        return pltpu.make_async_remote_copy(
            src_ref=rbuf.at[src],
            dst_ref=rbuf.at[src],
            send_sem=r_send.at[peer],
            recv_sem=r_recv.at[src],
            device_id=(me, peer),
            device_id_type=MESH,
        )

    for o in range(1, bands):
        across_rows(lax.rem(row + o, bands), row).start()
    for o in range(1, bands):
        peer = lax.rem(row + o, bands)
        across_rows(peer, peer).wait_recv()
    part = rbuf[0]
    for i in range(1, bands):
        part = part + rbuf[i]
    sbuf[me] = part

    def across_slab(peer, src):
        return pltpu.make_async_remote_copy(
            src_ref=sbuf.at[src],
            dst_ref=sbuf.at[src],
            send_sem=s_send.at[peer],
            recv_sem=s_recv.at[src],
            device_id=(peer, row),
            device_id_type=MESH,
        )

    for o in range(1, shards):
        across_slab(lax.rem(me + o, shards), me).start()
    for o in range(1, shards):
        place(lax.rem(me + o, shards)).start()
    for o in range(1, shards):
        peer = lax.rem(me + o, shards)
        across_slab(peer, peer).wait_recv()
    whole = sbuf[0]
    for i in range(1, shards):
        whole = whole + sbuf[i]

    lane_e = lax.broadcasted_iota(jnp.int32, (lanes, chan), 0)
    channel_e = lax.broadcasted_iota(jnp.int32, (lanes, chan), 1)

    def spread(matrix):
        return jnp.dot(whole, matrix, precision=HIGH, preferred_element_type=F32)

    cnt = spread((lane_e == 2 * GROUPS).astype(F32))
    mean = spread(member(channel_e, lane_e, 0)) / cnt
    var = spread(member(channel_e, lane_e, GROUPS)) / cnt - mean * mean
    scale = gain_ref[...] * (1.0 / jnp.sqrt(var + 1e-05))

    for copy, _, receives in halos:

        @pl.when(receives)
        def _(copy=copy):
            copy.wait_recv()

    @pl.when(me == 0)
    def _():
        idtab[pl.ds(0, LEAD), :] = jnp.full((LEAD, chan), -1, jnp.int32)

    ids = idtab[...]
    frame_mean = jnp.zeros(ids.shape, F32)
    frame_scale = jnp.zeros(ids.shape, F32)
    for c in range(CLIPS):
        frame_mean = jnp.where(ids == c, mean[c : c + 1, :], frame_mean)
        frame_scale = jnp.where(ids == c, scale[c : c + 1, :], frame_scale)
    mean_t[...] = frame_mean
    scale_t[...] = frame_scale

    shift = shift_ref[...]
    bsp = bsp_ref[...]
    btm = btm_ref[...]
    column = lax.broadcasted_iota(jnp.int32, (width, chan), 0)

    def spatial_frame(f, e):
        mu = mean_t[pl.ds(f + LEAD - BACK, 1), :]
        sc = scale_t[pl.ds(f + LEAD - BACK, 1), :]
        for i in range(band + 2):
            x = xin[f, pl.ds(i * width, width), :].astype(F32)
            v = (x - mu) * sc + shift
            half = 0.5 * v
            y = half + half * jnp.tanh(half)
            if i == 0:
                y = jnp.where(row > 0, y, 0.0)
            if i == band + 1:
                y = jnp.where(row < bands - 1, y, 0.0)
            rows_i = pl.ds(i * width, width)
            left = jnp.where(column == 0, 0.0, pltpu.roll(y, 1, 0))
            right = jnp.where(column == width - 1, 0.0, pltpu.roll(y, width - 1, 0))
            nbuf[rows_i, pl.ds(0, chan)] = left.astype(BF16)
            nbuf[rows_i, pl.ds(chan, chan)] = y.astype(BF16)
            nbuf[rows_i, pl.ds(2 * chan, chan)] = right.astype(BF16)
        for m in range(0, cells, 2 * width):
            size = min(2 * width, cells - m)
            acc = jnp.dot(nbuf[pl.ds(m, size), :], wsp_ref[0], preferred_element_type=F32)
            for a in (1, 2):
                acc = acc + jnp.dot(
                    nbuf[pl.ds(m + a * width, size), :], wsp_ref[a], preferred_element_type=F32
                )
            spat[e, pl.ds(m, size), :] = (acc + bsp).astype(BF16)

    def slot_frame(slot, entry):
        t = order_ref[slot]
        now = idtab[pl.ds(t + LEAD, 1), :]
        for m in range(0, cells, 2 * width):
            size = min(2 * width, cells - m)
            acc = xin[t + BACK, pl.ds(width + m, size), :].astype(F32) + btm
            for k in range(BACK + 1):
                term = jnp.dot(
                    spat[entry(t, k), pl.ds(m, size), :], wtm_ref[k], preferred_element_type=F32
                )
                if k > 0:
                    same = idtab[pl.ds(t + LEAD - k, 1), :] == now
                    term = jnp.where(same, term, 0.0)
                acc = acc + term
            sendbuf[slot, pl.ds(m, size), :] = acc.astype(BF16)

    def exchange(d, src, q):
        return pltpu.make_async_remote_copy(
            src_ref=sendbuf.at[d * per_peer + q],
            dst_ref=got_ref.at[src * per_peer + q],
            send_sem=x_send.at[d * per_peer + q],
            recv_sem=x_recv.at[src * per_peer + q],
            device_id=(d, row),
            device_id_type=MESH,
        )

    def target(i):
        return flipped(me, shards - 1 - i // per_peer, shards), lax.rem(i, per_peer)

    @pl.loop(0, direct)
    def _(i):
        d, q = target(i)
        slot = d * per_peer + q

        @pl.loop(0, BACK + 1)
        def _(k):
            spatial_frame(order_ref[slot] + BACK - k, count + BACK + k)

        slot_frame(slot, lambda t, k: count + BACK + k)
        exchange(d, me, q).start()

    @pl.loop(0, count + BACK)
    def _(f):
        spatial_frame(f, f)

    @pl.loop(direct, (shards - 1) * per_peer)
    def _(i):
        d, q = target(i)
        slot_frame(d * per_peer + q, lambda t, k: t + BACK - k)
        exchange(d, me, q).start()

    def keep(q):
        return pltpu.make_async_copy(
            sendbuf.at[me * per_peer + q], got_ref.at[me * per_peer + q], own_sem.at[q]
        )

    keep_pos = pltpu.make_async_copy(pos_ref.at[me], gotpos_ref.at[me], own_sem.at[per_peer])
    keep_pos.start()
    for q in range(per_peer):
        slot_frame(me * per_peer + q, lambda t, k: t + BACK - k)
        keep(q).start()

    for copy, sends, _ in halos:

        @pl.when(sends)
        def _(copy=copy):
            copy.wait_send()

    for o in range(1, bands):
        across_rows(lax.rem(row + o, bands), row).wait_send()
    for o in range(1, shards):
        across_slab(lax.rem(me + o, shards), me).wait_send()
    for o in range(1, shards):
        peer = lax.rem(me + o, shards)
        place(peer).wait_send()
        pltpu.make_async_remote_copy(
            src_ref=pos_ref.at[peer],
            dst_ref=gotpos_ref.at[peer],
            send_sem=p_send.at[peer],
            recv_sem=p_recv.at[peer],
            device_id=(peer, row),
            device_id_type=MESH,
        ).wait_recv()
    keep_pos.wait()
    for q in range(per_peer):
        keep(q).wait()

    @pl.loop(0, (shards - 1) * per_peer)
    def _(i):
        d, q = target(i)
        exchange(d, me, q).wait_send()
        exchange(d, d, q).wait_recv()


def lift_kernel(pos_ref, x_ref, w_ref, o_ref):
    del pos_ref
    o_ref[0] = jnp.dot(x_ref[0], w_ref[...], preferred_element_type=F32).astype(BF16)


def route(pack_dest, shards):
    count = pack_dest.shape[0]
    per_peer = count // shards
    target = pack_dest // count
    index = jnp.arange(count, dtype=jnp.int32)
    earlier = jnp.logical_and(target[:, None] == target[None, :], index[:, None] < index[None, :])
    slot_of = target * per_peer + jnp.sum(earlier.astype(jnp.int32), axis=0)
    selector = (slot_of[None, :] == index[:, None]).astype(jnp.int32)
    order = jnp.sum(selector * index[None, :], axis=1)
    position = jnp.sum(selector * (pack_dest % count)[None, :], axis=1)
    return order, position


def body(
    frames, clip_ids, norm_gain, norm_shift, w_spatial, b_spatial, w_time, b_time, w_lift, pack_dest
):
    count, band, width, chan = frames.shape
    lifted = w_lift.shape[1]
    cells = band * width
    shards = lax.axis_size("slab")
    bands = lax.axis_size("rows")
    per_peer = count // shards
    order, position = route(pack_dest, shards)
    pos = jnp.pad(position.reshape(shards, 1, per_peer), ((0, 0), (0, 0), (0, 128 - per_peer)))
    pos = jnp.broadcast_to(pos, (shards, 8, 128))
    ids = jnp.broadcast_to(clip_ids[:, None], (count, chan))
    vmem = pl.BlockSpec(memory_space=pltpu.VMEM)
    hbm = pl.BlockSpec(memory_space=pl.ANY)
    dma = pltpu.SemaphoreType.DMA
    got, gotpos = pl.pallas_call(
        functools.partial(block_kernel, shards, bands, width),
        out_shape=(
            jax.ShapeDtypeStruct((count, cells, chan), BF16),
            jax.ShapeDtypeStruct((shards, 8, 128), jnp.int32),
        ),
        in_specs=[pl.BlockSpec(memory_space=pltpu.SMEM), hbm] + [vmem] * 8,
        out_specs=(hbm, hbm),
        scratch_shapes=[
            pltpu.VMEM((count + BACK, cells + 2 * width, chan), BF16),
            pltpu.VMEM((LEAD + count, chan), jnp.int32),
            pltpu.VMEM((LEAD + count, chan), F32),
            pltpu.VMEM((LEAD + count, chan), F32),
            pltpu.VMEM((cells + 2 * width, 3 * chan), BF16),
            pltpu.VMEM((count + 2 * BACK + 1, cells, chan), BF16),
            pltpu.VMEM((count, cells, chan), BF16),
            pltpu.VMEM((bands, CLIPS, 128), F32),
            pltpu.VMEM((shards, CLIPS, 128), F32),
            dma((count,)),
            dma((6,)),
            dma((6,)),
            dma((bands,)),
            dma((bands,)),
            dma((shards,)),
            dma((shards,)),
            dma((shards,)),
            dma((shards,)),
            dma((count,)),
            dma((count,)),
            dma((per_peer + 1,)),
        ],
        compiler_params=pltpu.CompilerParams(
            collective_id=0, has_side_effects=True, vmem_limit_bytes=44 * 1024 * 1024
        ),
        name="block",
    )(
        order,
        frames.reshape(count, cells, chan),
        ids,
        pos,
        norm_gain.reshape(1, chan),
        norm_shift.reshape(1, chan),
        w_spatial.reshape(3, 3 * chan, chan),
        b_spatial.reshape(1, chan),
        w_time,
        b_time.reshape(1, chan),
    )
    where_to = gotpos[:, 0, :per_peer].reshape(count)
    packed = pl.pallas_call(
        lift_kernel,
        out_shape=jax.ShapeDtypeStruct((count, cells, lifted), BF16),
        grid_spec=pltpu.PrefetchScalarGridSpec(
            num_scalar_prefetch=1,
            grid=(count,),
            in_specs=[
                pl.BlockSpec((1, cells, chan), lambda s, p: (s, 0, 0)),
                pl.BlockSpec((chan, lifted), lambda s, p: (0, 0)),
            ],
            out_specs=pl.BlockSpec((1, cells, lifted), lambda s, p: (p[s], 0, 0)),
        ),
        compiler_params=pltpu.CompilerParams(vmem_limit_bytes=16 * 1024 * 1024),
        name="lift",
    )(where_to, got, w_lift)
    return packed.reshape(count, band, width, lifted)


def solution(mesh):
    in_specs = (
        P("slab", "rows", None, None),
        P("slab"),
        P(),
        P(),
        P(),
        P(),
        P(),
        P(),
        P(),
        P("slab"),
    )
    out_specs = P("slab", "rows", None, None)
    return jax.shard_map(body, mesh=mesh, in_specs=in_specs, out_specs=out_specs, check_vma=False)
```

time: 311 us -> 150 us (0.48)
  Pallas kernels: 0 us -> 136 us
  waiting for transfers between devices: 99.7 us -> 0 us
  matrix products: 97.8 us -> 0 us
  blocking collectives: 42.2 us -> 0 us
  local copies, waits for them, and re-layouts: 36.2 us -> 12.3 us
  starting transfers between devices: 21.1 us -> 0 us
  other arithmetic: 13.3 us -> 0.88 us
    pallas_call x0 -> x2, Pallas kernels: none -> 136 us  [the longest x1 127 us: body(): pl.pallas_call(functools.partial(block_kernel, shards, bands, width), out...]
    dot_general x19 -> x0, matrix products: 97.8 us -> none  [the longest x9 59.8 us: body(): jnp.einsum('trwc,cd->trwd', padded[:, a:a + band, b:b + width], w_spatial...]
    all_to_all x2 -> x0, waiting for transfers between devices: 93.2 us -> none  [the longest x1 93.2 us: body(): lax.all_to_all(outgoing, 'slab', split_axis=0, concat_axis=0, tiled=True)]
    psum x1 -> x0, blocking collectives: 42.2 us -> none  [body(): lax.psum((jnp.dot(onehot.T, sums, precision=lax.Precision.HIGHEST), jnp.d...]
    reshape x3 -> x1, local copies, waits for them, and re-layouts: 23 us -> 0.08 us  [body(): position.reshape(shards, 1, per_peer)]
    ppermute x4 -> x0, starting transfers between devices: 11 us -> none  [the longest x2 8.35 us: shifted(): return lax.ppermute(block, axis, route)]
    all_to_all x2 -> x0, starting transfers between devices: 10.1 us -> none  [the longest x1 6.52 us: body(): lax.all_to_all(outgoing, 'slab', split_axis=0, concat_axis=0, tiled=True)]
    unnamed x22 -> x20, local copies, waits for them, and re-layouts: 2.06 us -> 11.4 us
  transfers between devices with their start and end apart: 6 -> 0, of which waited for: 2 -> 0; matrix products, arithmetic and copies ran while one was open for 34% -> 0% of each run, Pallas kernels for 0% -> 0%
where the time goes in v1:
time: 150 us; the launch traced here: 149 us
  Pallas kernels  136 us (91%)
  local copies, waits for them, and re-layouts  12.3 us (8%)
    pallas_call x1, Pallas kernels, body(): pl.pallas_call(functools.partial(block_kernel, shards, bands, width), out...  127 us
    unnamed x20, local copies, waits for them, and re-layouts  11.4 us
    pallas_call x1, Pallas kernels, body(): pl.pallas_call(lift_kernel, out_shape=jax.ShapeDtypeStruct((count, cells,...  9.56 us

profile of v1, /device:TPU:0, one launch (start us, length us, event | category | flops | bytes accessed | tf_op | source)
XLA Modules:
  0.0 149.4 jit_solution(12232040244584878230)
XLA Ops:
  0.0 0.7 and_select_fusion.1
  0.7 0.1 convert_reduce_fusion
  0.8 0.1 select_reduce_fusion
  0.9 0.1 reshape.30
  1.0 0.7 broadcast_in_dim.6.ids_ref
  1.7 0.0 copy-start
  1.7 2.2 %copy-done = bf16[16,4,128,256]{3,2,1,0:T(8,128)(2,1)S(1)} copy-done((bf16[16,4,128,256]{3,2,1,0:T(8,128)(2,1)S(1)}, bf16[16,4,128,256]{3,2,1,0:T(8,128)(2,1)}, u32[]{:S(2)}) %copy-start) | copy-done | bytes 4194328
  3.9 0.0 copy-start.3
  3.9 1.3 copy-done.3
  5.2 0.0 copy-start.4
  5.2 1.0 copy-done.4
  6.2 0.0 copy-start.6
  6.2 0.7 copy-done.6
  6.8 0.0 copy-start.7
  6.8 0.7 copy-done.7
  7.5 0.0 copy-start.8
  7.5 0.7 copy-done.8
  8.2 0.0 copy-start.9
  8.2 0.7 copy-done.9
  8.9 0.0 copy-start.5
  8.9 126.6 %block.1 = (bf16[16,512,256]{2,1,0:T(8,128)(2,1)S(1)}, s32[8,8,128]{2,1,0:T(8,128)S(1)}) custom-call(s32[16]{0:T(128)S(1)} %get-tuple-element.10.order_ref, bf16[16,512,256]{2,1,0:T(8,128)(2,1)S(1)} %bitcast.9, s32[16,256]{1,0:T(8,128)S(1)} %broadcast_in_dim.6.ids_ref, s32[8,8,128]{2,1,0:T(8,128)S(1)} %broadcast_in_dim.8.pos_ref, f32[1,256]{1,0:T(1,128)S(1)} %bitcast.11, ...), custom_call_target="tpu_custom_call" | custom-call | tf_op jit(solution)/shard_map/block/pallas_call | solution.py:439
  135.5 0.0 copy-start.1
  135.5 2.0 %copy-done.1 = bf16[16,512,256]{2,1,0:T(8,128)(2,1)} copy-done((bf16[16,512,256]{2,1,0:T(8,128)(2,1)}, bf16[16,512,256]{2,1,0:T(8,128)(2,1)S(1)}, u32[]{:S(2)}) %copy-start.1) | copy-done | bytes 4194328
  137.5 0.1 reshape_squeeze.3.pos_ref
  137.6 0.0 copy-done.5
  137.6 0.0 copy-start.2
  137.6 2.2 %copy-done.2 = bf16[16,512,256]{2,1,0:T(8,128)(2,1)S(1)} copy-done((bf16[16,512,256]{2,1,0:T(8,128)(2,1)S(1)}, bf16[16,512,256]{2,1,0:T(8,128)(2,1)}, u32[]{:S(2)}) %copy-start.2) | copy-done | bytes 4194328
  139.8 9.6 %lift.1 = bf16[16,512,512]{2,1,0:T(8,128)(2,1)} custom-call(s32[16]{0:T(128)S(1)} %reshape_squeeze.3.pos_ref, bf16[16,512,256]{2,1,0:T(8,128)(2,1)S(1)} %copy-done.2, bf16[256,512]{1,0:T(8,128)(2,1)S(1)} %copy-done.5), custom_call_target="tpu_custom_call" | custom-call | tf_op jit(solution)/shard_map/lift/pallas_call | solution.py:487
  (4 shorter events, 0.0 us)
Async XLA Ops:
  1.7 2.2 %copy-start = (bf16[16,4,128,256]{3,2,1,0:T(8,128)(2,1)S(1)}, bf16[16,4,128,256]{3,2,1,0:T(8,128)(2,1)}, u32[]{:S(2)}) copy-start(bf16[16,4,128,256]{3,2,1,0:T(8,128)(2,1)} %param.10) | copy-start | bytes 12582916
  3.9 1.3 copy-start.3
  5.2 1.0 copy-start.4
  6.2 0.7 copy-start.6
  6.8 0.7 copy-start.7
  7.5 0.7 copy-start.8
  8.2 0.7 copy-start.9
  8.9 128.7 %copy-start.5 = (bf16[256,512]{1,0:T(8,128)(2,1)S(1)}, bf16[256,512]{1,0:T(8,128)(2,1)}, u32[]{:S(2)}) copy-start(bf16[256,512]{1,0:T(8,128)(2,1)} %w_ref.1) | copy-start | bytes 786436
  135.5 2.0 %copy-start.1 = (bf16[16,512,256]{2,1,0:T(8,128)(2,1)}, bf16[16,512,256]{2,1,0:T(8,128)(2,1)S(1)}, u32[]{:S(2)}) copy-start(bf16[16,512,256]{2,1,0:T(8,128)(2,1)S(1)} %get-tuple-element.8.x_ref) | copy-start | bytes 12582916
  137.6 2.2 %copy-start.2 = (bf16[16,512,256]{2,1,0:T(8,128)(2,1)S(1)}, bf16[16,512,256]{2,1,0:T(8,128)(2,1)}, u32[]{:S(2)}) copy-start(bf16[16,512,256]{2,1,0:T(8,128)(2,1)} %copy-done.1) | copy-start | bytes 12582916

commit v2 on v1

--- a/solution.py
+++ b/solution.py
@@ -11,7 +11,7 @@
 CLIPS = 16
 BACK = 2
 LEAD = 8
-DIRECT = 4
+DIRECT = 5
 MESH = pl.DeviceIdType.MESH
 HIGH = lax.Precision.HIGHEST
 F32 = jnp.float32
@@ -34,12 +34,12 @@
     frames_ref,
     ids_ref,
     pos_ref,
-    gain_ref,
-    shift_ref,
-    wsp_ref,
-    bsp_ref,
-    wtm_ref,
-    btm_ref,
+    gain_hbm,
+    shift_hbm,
+    bsp_hbm,
+    btm_hbm,
+    wsp_hbm,
+    wtm_hbm,
     got_ref,
     gotpos_ref,
     xin,
@@ -51,7 +51,11 @@
     sendbuf,
     rbuf,
     sbuf,
+    rows_v,
+    wsp_ref,
+    wtm_ref,
     load_sem,
+    param_sem,
     halo_send,
     halo_recv,
     r_send,
@@ -70,6 +74,7 @@
     band = cells // width
     me = lax.axis_index("slab")
     row = lax.axis_index("rows")
+    group = BACK + 1
     direct = min(DIRECT, (shards - 1) * per_peer)
 
     def load(t):
@@ -80,6 +85,22 @@
     @pl.loop(0, count)
     def _(t):
         load(t).start()
+
+    params = [
+        pltpu.make_async_copy(src, dst, param_sem.at[i])
+        for i, (src, dst) in enumerate(
+            (
+                (gain_hbm, rows_v.at[0]),
+                (shift_hbm, rows_v.at[1]),
+                (bsp_hbm, rows_v.at[2]),
+                (btm_hbm, rows_v.at[3]),
+                (wsp_hbm, wsp_ref),
+                (wtm_hbm, wtm_ref),
+            )
+        )
+    ]
+    for copy in params:
+        copy.start()
 
     barrier = pltpu.get_barrier_semaphore()
     for o in range(1, bands):
@@ -252,10 +273,12 @@
     def spread(matrix):
         return jnp.dot(whole, matrix, precision=HIGH, preferred_element_type=F32)
 
+    for copy in params:
+        copy.wait()
     cnt = spread((lane_e == 2 * GROUPS).astype(F32))
     mean = spread(member(channel_e, lane_e, 0)) / cnt
     var = spread(member(channel_e, lane_e, GROUPS)) / cnt - mean * mean
-    scale = gain_ref[...] * (1.0 / jnp.sqrt(var + 1e-05))
+    scale = rows_v[0] * (1.0 / jnp.sqrt(var + 1e-05))
 
     for copy, _, receives in halos:
 
@@ -276,12 +299,12 @@
     mean_t[...] = frame_mean
     scale_t[...] = frame_scale
 
-    shift = shift_ref[...]
-    bsp = bsp_ref[...]
-    btm = btm_ref[...]
+    shift = rows_v[1]
+    bsp = rows_v[2]
+    btm = rows_v[3]
     column = lax.broadcasted_iota(jnp.int32, (width, chan), 0)
 
-    def spatial_frame(f, e):
+    def normalise(f, place_at):
         mu = mean_t[pl.ds(f + LEAD - BACK, 1), :]
         sc = scale_t[pl.ds(f + LEAD - BACK, 1), :]
         for i in range(band + 2):
@@ -293,36 +316,37 @@
                 y = jnp.where(row > 0, y, 0.0)
             if i == band + 1:
                 y = jnp.where(row < bands - 1, y, 0.0)
-            rows_i = pl.ds(i * width, width)
             left = jnp.where(column == 0, 0.0, pltpu.roll(y, 1, 0))
             right = jnp.where(column == width - 1, 0.0, pltpu.roll(y, width - 1, 0))
-            nbuf[rows_i, pl.ds(0, chan)] = left.astype(BF16)
-            nbuf[rows_i, pl.ds(chan, chan)] = y.astype(BF16)
-            nbuf[rows_i, pl.ds(2 * chan, chan)] = right.astype(BF16)
-        for m in range(0, cells, 2 * width):
-            size = min(2 * width, cells - m)
-            acc = jnp.dot(nbuf[pl.ds(m, size), :], wsp_ref[0], preferred_element_type=F32)
-            for a in (1, 2):
-                acc = acc + jnp.dot(
-                    nbuf[pl.ds(m + a * width, size), :], wsp_ref[a], preferred_element_type=F32
-                )
-            spat[e, pl.ds(m, size), :] = (acc + bsp).astype(BF16)
+            nbuf[i, place_at, :, pl.ds(0, chan)] = left.astype(BF16)
+            nbuf[i, place_at, :, pl.ds(chan, chan)] = y.astype(BF16)
+            nbuf[i, place_at, :, pl.ds(2 * chan, chan)] = right.astype(BF16)
+
+    def convolve(entry):
+        size = band * group * width
+        acc = jnp.zeros((size, chan), F32) + bsp
+        for a in range(3):
+            acc = acc + jnp.dot(
+                nbuf[pl.ds(a, band)].reshape(size, 3 * chan),
+                wsp_ref[a],
+                preferred_element_type=F32,
+            )
+        out = acc.astype(BF16).reshape(band, group, width, chan)
+        for i in range(band):
+            for g in range(group):
+                spat[entry + g, pl.ds(i * width, width), :] = out[i, g]
 
     def slot_frame(slot, entry):
         t = order_ref[slot]
         now = idtab[pl.ds(t + LEAD, 1), :]
-        for m in range(0, cells, 2 * width):
-            size = min(2 * width, cells - m)
-            acc = xin[t + BACK, pl.ds(width + m, size), :].astype(F32) + btm
-            for k in range(BACK + 1):
-                term = jnp.dot(
-                    spat[entry(t, k), pl.ds(m, size), :], wtm_ref[k], preferred_element_type=F32
-                )
-                if k > 0:
-                    same = idtab[pl.ds(t + LEAD - k, 1), :] == now
-                    term = jnp.where(same, term, 0.0)
-                acc = acc + term
-            sendbuf[slot, pl.ds(m, size), :] = acc.astype(BF16)
+        acc = xin[t + BACK, pl.ds(width, cells), :].astype(F32) + btm
+        for k in range(BACK + 1):
+            term = jnp.dot(spat[entry(t, k)], wtm_ref[k], preferred_element_type=F32)
+            if k > 0:
+                same = idtab[pl.ds(t + LEAD - k, 1), :] == now
+                term = jnp.where(same, term, 0.0)
+            acc = acc + term
+        sendbuf[slot] = acc.astype(BF16)
 
     def exchange(d, src, q):
         return pltpu.make_async_remote_copy(
@@ -344,14 +368,20 @@
 
         @pl.loop(0, BACK + 1)
         def _(k):
-            spatial_frame(order_ref[slot] + BACK - k, count + BACK + k)
+            normalise(order_ref[slot] + BACK - k, k)
+
+        convolve(count + BACK)
 
         slot_frame(slot, lambda t, k: count + BACK + k)
         exchange(d, me, q).start()
 
-    @pl.loop(0, count + BACK)
-    def _(f):
-        spatial_frame(f, f)
+    @pl.loop(0, (count + BACK) // group)
+    def _(g):
+        @pl.loop(0, group)
+        def _(k):
+            normalise(g * group + k, k)
+
+        convolve(g * group)
 
     @pl.loop(direct, (shards - 1) * per_peer)
     def _(i):
@@ -402,9 +432,33 @@
         exchange(d, d, q).wait_recv()
 
 
-def lift_kernel(pos_ref, x_ref, w_ref, o_ref):
-    del pos_ref
-    o_ref[0] = jnp.dot(x_ref[0], w_ref[...], preferred_element_type=F32).astype(BF16)
+def lift_kernel(pos_ref, x_hbm, w_hbm, o_hbm, x, w, out, x_sem, w_sem, out_sem):
+    count = x.shape[0]
+
+    def load(s):
+        return pltpu.make_async_copy(x_hbm.at[s], x.at[s], x_sem.at[s])
+
+    def store(s):
+        return pltpu.make_async_copy(out.at[s], o_hbm.at[pos_ref[s]], out_sem.at[s])
+
+    weights = pltpu.make_async_copy(w_hbm, w, w_sem)
+    weights.start()
+
+    @pl.loop(0, count)
+    def _(s):
+        load(s).start()
+
+    weights.wait()
+
+    @pl.loop(0, count)
+    def _(s):
+        load(s).wait()
+        out[s] = jnp.dot(x[s], w[...], preferred_element_type=F32).astype(BF16)
+        store(s).start()
+
+    @pl.loop(0, count)
+    def _(s):
+        store(s).wait()
 
 
 def route(pack_dest, shards):
@@ -442,19 +496,23 @@
             jax.ShapeDtypeStruct((count, cells, chan), BF16),
             jax.ShapeDtypeStruct((shards, 8, 128), jnp.int32),
         ),
-        in_specs=[pl.BlockSpec(memory_space=pltpu.SMEM), hbm] + [vmem] * 8,
+        in_specs=[pl.BlockSpec(memory_space=pltpu.SMEM), hbm, vmem, vmem] + [hbm] * 6,
         out_specs=(hbm, hbm),
         scratch_shapes=[
             pltpu.VMEM((count + BACK, cells + 2 * width, chan), BF16),
             pltpu.VMEM((LEAD + count, chan), jnp.int32),
             pltpu.VMEM((LEAD + count, chan), F32),
             pltpu.VMEM((LEAD + count, chan), F32),
-            pltpu.VMEM((cells + 2 * width, 3 * chan), BF16),
+            pltpu.VMEM((band + 2, BACK + 1, width, 3 * chan), BF16),
             pltpu.VMEM((count + 2 * BACK + 1, cells, chan), BF16),
             pltpu.VMEM((count, cells, chan), BF16),
             pltpu.VMEM((bands, CLIPS, 128), F32),
             pltpu.VMEM((shards, CLIPS, 128), F32),
+            pltpu.VMEM((4, 1, chan), F32),
+            pltpu.VMEM((3, 3 * chan, chan), BF16),
+            pltpu.VMEM((BACK + 1, chan, chan), BF16),
             dma((count,)),
+            dma((6,)),
             dma((6,)),
             dma((6,)),
             dma((bands,)),
@@ -468,7 +526,7 @@
             dma((per_peer + 1,)),
         ],
         compiler_params=pltpu.CompilerParams(
-            collective_id=0, has_side_effects=True, vmem_limit_bytes=44 * 1024 * 1024
+            collective_id=0, has_side_effects=True, vmem_limit_bytes=60 * 1024 * 1024
         ),
         name="block",
     )(
@@ -478,25 +536,26 @@
         pos,
         norm_gain.reshape(1, chan),
         norm_shift.reshape(1, chan),
+        b_spatial.reshape(1, chan),
+        b_time.reshape(1, chan),
         w_spatial.reshape(3, 3 * chan, chan),
-        b_spatial.reshape(1, chan),
         w_time,
-        b_time.reshape(1, chan),
     )
     where_to = gotpos[:, 0, :per_peer].reshape(count)
     packed = pl.pallas_call(
         lift_kernel,
         out_shape=jax.ShapeDtypeStruct((count, cells, lifted), BF16),
-        grid_spec=pltpu.PrefetchScalarGridSpec(
-            num_scalar_prefetch=1,
-            grid=(count,),
-            in_specs=[
-                pl.BlockSpec((1, cells, chan), lambda s, p: (s, 0, 0)),
-                pl.BlockSpec((chan, lifted), lambda s, p: (0, 0)),
-            ],
-            out_specs=pl.BlockSpec((1, cells, lifted), lambda s, p: (p[s], 0, 0)),
-        ),
-        compiler_params=pltpu.CompilerParams(vmem_limit_bytes=16 * 1024 * 1024),
+        in_specs=[pl.BlockSpec(memory_space=pltpu.SMEM), hbm, hbm],
+        out_specs=hbm,
+        scratch_shapes=[
+            pltpu.VMEM((count, cells, chan), BF16),
+            pltpu.VMEM((chan, lifted), BF16),
+            pltpu.VMEM((count, cells, lifted), BF16),
+            dma((count,)),
+            dma,
+            dma((count,)),
+        ],
+        compiler_params=pltpu.CompilerParams(vmem_limit_bytes=60 * 1024 * 1024),
         name="lift",
     )(where_to, got, w_lift)
     return packed.reshape(count, band, width, lifted)

time: 150 us -> 139 us (0.927)
  local copies, waits for them, and re-layouts: 12.3 us -> 3.42 us
  Pallas kernels: 136 us -> 134 us
    unnamed x20 -> x0, local copies, waits for them, and re-layouts: 11.4 us -> none
    pallas_call x1, Pallas kernels: 9.56 us -> 7.6 us  [body(): pl.pallas_call(lift_kernel, out_shape=jax.ShapeDtypeStruct((count, cells,...]
where the time goes in v2:
time: 139 us
  Pallas kernels  134 us (96%)
  local copies, waits for them, and re-layouts  3.42 us (2%)
    pallas_call x1, Pallas kernels, body(): pl.pallas_call(functools.partial(block_kernel, shards, bands, width), out...  126 us
    pallas_call x1, Pallas kernels, body(): pl.pallas_call(lift_kernel, out_shape=jax.ShapeDtypeStruct((count, cells,...  7.6 us

profile of v2, /device:TPU:0, one launch (start us, length us, event | category | flops | bytes accessed | tf_op | source)
XLA Modules:
  0.0 138.8 jit_solution(5030142998979362595)
XLA Ops:
  0.0 0.7 and_select_fusion.1
  0.7 0.1 convert_reduce_fusion
  0.8 0.6 select_reduce_fusion
  1.4 0.1 reshape.30
  1.5 1.3 broadcast_in_dim.6.ids_ref
  2.8 0.6 broadcast_in_dim.8.pos_ref
  3.4 126.4 %block.1 = (bf16[16,512,256]{2,1,0:T(8,128)(2,1)}, s32[8,8,128]{2,1,0:T(8,128)}) custom-call(s32[16]{0:T(128)} %get-tuple-element.10.order_ref, bf16[16,512,256]{2,1,0:T(8,128)(2,1)} %bitcast.9, s32[16,256]{1,0:T(8,128)} %broadcast_in_dim.6.ids_ref, s32[8,8,128]{2,1,0:T(8,128)} %broadcast_in_dim.8.pos_ref, f32[1,256]{1,0:T(1,128)} %bitcast.11, ...), custom_call_target="tpu_custom_call" | custom-call | tf_op jit(solution)/shard_map/block/pallas_call | solution.py:493
  129.8 0.8 slice_reduce_fusion
  130.6 0.6 reshape_squeeze.3.pos_ref
  131.2 7.6 %lift.1 = bf16[16,512,512]{2,1,0:T(8,128)(2,1)} custom-call(s32[16]{0:T(128)} %reshape_squeeze.3.pos_ref, bf16[16,512,256]{2,1,0:T(8,128)(2,1)} %get-tuple-element.8.x_hbm, bf16[256,512]{1,0:T(8,128)(2,1)} %w_hbm.1), custom_call_target="tpu_custom_call" | custom-call | tf_op jit(solution)/shard_map/lift/pallas_call | solution.py:545
  (2 shorter events, 0.0 us)

commit v3 on v2

--- a/solution.py
+++ b/solution.py
@@ -11,7 +11,7 @@
 CLIPS = 16
 BACK = 2
 LEAD = 8
-DIRECT = 5
+DIRECT = 6
 MESH = pl.DeviceIdType.MESH
 HIGH = lax.Precision.HIGHEST
 F32 = jnp.float32
@@ -31,9 +31,9 @@
     bands,
     width,
     order_ref,
+    position_ref,
+    clip_ref,
     frames_ref,
-    ids_ref,
-    pos_ref,
     gain_hbm,
     shift_hbm,
     bsp_hbm,
@@ -43,6 +43,7 @@
     got_ref,
     gotpos_ref,
     xin,
+    pos_ref,
     idtab,
     mean_t,
     scale_t,
@@ -119,6 +120,15 @@
                 device_id=(lax.rem(me + a, shards), lax.rem(row + b, bands)),
                 device_id_type=MESH,
             )
+
+    for t in range(count):
+        idtab[LEAD + t : LEAD + t + 1, :] = jnp.full((1, chan), clip_ref[t], jnp.int32)
+    pos_lane = lax.broadcasted_iota(jnp.int32, (1, 128), 1)
+    for d in range(shards):
+        line = jnp.zeros((1, 128), jnp.int32)
+        for q in range(per_peer):
+            line = jnp.where(pos_lane == q, position_ref[d * per_peer + q], line)
+        pos_ref[d] = line
     pl.semaphore_wait(barrier, bands - 1 + shards - 1 + 4)
 
     top = pl.ds(0, width)
@@ -169,7 +179,7 @@
             row < bands - 1,
         ),
         (
-            halo(5, ids_ref.at[pl.ds(count - LEAD, LEAD)], idtab.at[pl.ds(0, LEAD)], up_slab, row),
+            halo(5, idtab.at[pl.ds(count, LEAD)], idtab.at[pl.ds(0, LEAD)], up_slab, row),
             me < shards - 1,
             me > 0,
         ),
@@ -190,7 +200,6 @@
             device_id_type=MESH,
         )
 
-    idtab[pl.ds(LEAD, count), :] = ids_ref[...]
     clip_row = lax.broadcasted_iota(jnp.int32, (CLIPS, chan), 0)
     zero = jnp.zeros((CLIPS, chan), F32)
 
@@ -200,7 +209,7 @@
         x = xin[t + BACK, pl.ds(width, cells), :].astype(F32)
         one = jnp.sum(x, axis=0, keepdims=True)
         two = jnp.sum(x * x, axis=0, keepdims=True)
-        mine = clip_row == ids_ref[pl.ds(t, 1), :]
+        mine = clip_row == idtab[pl.ds(t + LEAD, 1), :]
         return (
             total + jnp.where(mine, one, 0.0),
             squares + jnp.where(mine, two, 0.0),
@@ -358,7 +367,14 @@
             device_id_type=MESH,
         )
 
+    slots = (shards - 1) * per_peer
+    far = shards // 2 * per_peer
+
     def target(i):
+        if per_peer <= 2:
+            inside = 1 - i // (slots // 2 * 2)
+            i = i + inside * lax.rem(row, 2) * (1 - 2 * lax.rem(i, 2))
+            i = i // 2 + (1 - lax.rem(i, 2)) * (far - 1)
         return flipped(me, shards - 1 - i // per_peer, shards), lax.rem(i, per_peer)
 
     @pl.loop(0, direct)
@@ -434,12 +450,14 @@
 
 def lift_kernel(pos_ref, x_hbm, w_hbm, o_hbm, x, w, out, x_sem, w_sem, out_sem):
     count = x.shape[0]
+    per_peer = count // pos_ref.shape[0]
 
     def load(s):
         return pltpu.make_async_copy(x_hbm.at[s], x.at[s], x_sem.at[s])
 
     def store(s):
-        return pltpu.make_async_copy(out.at[s], o_hbm.at[pos_ref[s]], out_sem.at[s])
+        p = pos_ref[s // per_peer, 0, lax.rem(s, per_peer)]
+        return pltpu.make_async_copy(out.at[s], o_hbm.at[p], out_sem.at[s])
 
     weights = pltpu.make_async_copy(w_hbm, w, w_sem)
     weights.start()
@@ -484,22 +502,20 @@
     bands = lax.axis_size("rows")
     per_peer = count // shards
     order, position = route(pack_dest, shards)
-    pos = jnp.pad(position.reshape(shards, 1, per_peer), ((0, 0), (0, 0), (0, 128 - per_peer)))
-    pos = jnp.broadcast_to(pos, (shards, 8, 128))
-    ids = jnp.broadcast_to(clip_ids[:, None], (count, chan))
-    vmem = pl.BlockSpec(memory_space=pltpu.VMEM)
+    smem = pl.BlockSpec(memory_space=pltpu.SMEM)
     hbm = pl.BlockSpec(memory_space=pl.ANY)
     dma = pltpu.SemaphoreType.DMA
     got, gotpos = pl.pallas_call(
         functools.partial(block_kernel, shards, bands, width),
         out_shape=(
             jax.ShapeDtypeStruct((count, cells, chan), BF16),
-            jax.ShapeDtypeStruct((shards, 8, 128), jnp.int32),
-        ),
-        in_specs=[pl.BlockSpec(memory_space=pltpu.SMEM), hbm, vmem, vmem] + [hbm] * 6,
+            jax.ShapeDtypeStruct((shards, 1, 128), jnp.int32),
+        ),
+        in_specs=[smem] * 3 + [hbm] * 7,
         out_specs=(hbm, hbm),
         scratch_shapes=[
             pltpu.VMEM((count + BACK, cells + 2 * width, chan), BF16),
+            pltpu.VMEM((shards, 1, 128), jnp.int32),
             pltpu.VMEM((LEAD + count, chan), jnp.int32),
             pltpu.VMEM((LEAD + count, chan), F32),
             pltpu.VMEM((LEAD + count, chan), F32),
@@ -531,9 +547,9 @@
         name="block",
     )(
         order,
+        position,
+        clip_ids,
         frames.reshape(count, cells, chan),
-        ids,
-        pos,
         norm_gain.reshape(1, chan),
         norm_shift.reshape(1, chan),
         b_spatial.reshape(1, chan),
@@ -541,11 +557,10 @@
         w_spatial.reshape(3, 3 * chan, chan),
         w_time,
     )
-    where_to = gotpos[:, 0, :per_peer].reshape(count)
     packed = pl.pallas_call(
         lift_kernel,
         out_shape=jax.ShapeDtypeStruct((count, cells, lifted), BF16),
-        in_specs=[pl.BlockSpec(memory_space=pltpu.SMEM), hbm, hbm],
+        in_specs=[smem, hbm, hbm],
         out_specs=hbm,
         scratch_shapes=[
             pltpu.VMEM((count, cells, chan), BF16),
@@ -557,7 +572,7 @@
         ],
         compiler_params=pltpu.CompilerParams(vmem_limit_bytes=60 * 1024 * 1024),
         name="lift",
-    )(where_to, got, w_lift)
+    )(gotpos, got, w_lift)
     return packed.reshape(count, band, width, lifted)
 
 

time: 139 us -> 133 us (0.957)
  local copies, waits for them, and re-layouts: 3.42 us -> 0 us
  Pallas kernels: 134 us -> 132 us
    pallas_call x1, Pallas kernels: 126 us -> 124 us  [body(): pl.pallas_call(functools.partial(block_kernel, shards, bands, width), out...]
    broadcast_in_dim x3 -> x0, local copies, waits for them, and re-layouts: 1.97 us -> none  [the longest x1 1.34 us: body(): ids = jnp.broadcast_to(clip_ids[:, None], (count, chan))]
where the time goes in v3:
time: 133 us
  Pallas kernels  132 us (99%)
  other arithmetic  1.42 us (1%)
    pallas_call x1, Pallas kernels, body(): pl.pallas_call(functools.partial(block_kernel, shards, bands, width), out...  124 us
    pallas_call x1, Pallas kernels, body(): pl.pallas_call(lift_kernel, out_shape=jax.ShapeDtypeStruct((count, cells,...  7.67 us

profile of v3, /device:TPU:0, one launch (start us, length us, event | category | flops | bytes accessed | tf_op | source)
XLA Modules:
  0.0 133.1 jit_solution(17603938635409503840)
XLA Ops:
  0.0 0.7 and_select_fusion.1
  0.7 0.1 convert_reduce_fusion
  0.8 0.7 select_reduce_fusion
  1.4 124.0 %block.1 = (bf16[16,512,256]{2,1,0:T(8,128)(2,1)}, s32[8,1,128]{2,1,0:T(1,128)}) custom-call(s32[16]{0:T(128)} %get-tuple-element.10.order_ref, s32[16]{0:T(128)} %get-tuple-element.9.position_ref, s32[16]{0:T(128)} %clip_ref.1, bf16[16,512,256]{2,1,0:T(8,128)(2,1)} %bitcast.7, f32[1,256]{1,0:T(1,128)} %bitcast.9, f32[1,256]{1,0:T(1,128)} %bitcast.10, ...), custom_call_target="tpu_custom_call" | custom-call | tf_op jit(solution)/shard_map/block/pallas_call | solution.py:508
  125.5 7.7 %lift.1 = bf16[16,512,512]{2,1,0:T(8,128)(2,1)} custom-call(s32[8,1,128]{2,1,0:T(1,128)} %get-tuple-element.7.pos_ref, bf16[16,512,256]{2,1,0:T(8,128)(2,1)} %get-tuple-element.8.x_hbm, bf16[256,512]{1,0:T(8,128)(2,1)} %w_hbm.1), custom_call_target="tpu_custom_call" | custom-call | tf_op jit(solution)/shard_map/lift/pallas_call | solution.py:560
  (1 shorter events, 0.0 us)

commit v4 on v3

--- a/solution.py
+++ b/solution.py
@@ -11,7 +11,7 @@
 CLIPS = 16
 BACK = 2
 LEAD = 8
-DIRECT = 6
+DIRECT = 5
 MESH = pl.DeviceIdType.MESH
 HIGH = lax.Precision.HIGHEST
 F32 = jnp.float32
@@ -112,14 +112,6 @@
         pl.semaphore_signal(
             barrier, inc=1, device_id=(lax.rem(me + o, shards), row), device_id_type=MESH
         )
-    for a in (1, shards - 1):
-        for b in (1, bands - 1):
-            pl.semaphore_signal(
-                barrier,
-                inc=1,
-                device_id=(lax.rem(me + a, shards), lax.rem(row + b, bands)),
-                device_id_type=MESH,
-            )
 
     for t in range(count):
         idtab[LEAD + t : LEAD + t + 1, :] = jnp.full((1, chan), clip_ref[t], jnp.int32)
@@ -129,7 +121,7 @@
         for q in range(per_peer):
             line = jnp.where(pos_lane == q, position_ref[d * per_peer + q], line)
         pos_ref[d] = line
-    pl.semaphore_wait(barrier, bands - 1 + shards - 1 + 4)
+    pl.semaphore_wait(barrier, bands - 1 + shards - 1)
 
     top = pl.ds(0, width)
     bottom = pl.ds(width + cells, width)
@@ -159,13 +151,13 @@
             me > 0,
         ),
         (
-            halo(1, frames_ref.at[tail, last], xin.at[prior, top], up_slab, up_row),
-            jnp.logical_and(me < shards - 1, row < bands - 1),
+            halo(1, xin.at[prior, pl.ds(cells, width)], xin.at[prior, top], me, up_row),
+            jnp.logical_and(me > 0, row < bands - 1),
             jnp.logical_and(me > 0, row > 0),
         ),
         (
-            halo(2, frames_ref.at[tail, first], xin.at[prior, bottom], up_slab, down_row),
-            jnp.logical_and(me < shards - 1, row > 0),
+            halo(2, xin.at[prior, pl.ds(width, width)], xin.at[prior, bottom], me, down_row),
+            jnp.logical_and(me > 0, row > 0),
             jnp.logical_and(me > 0, row < bands - 1),
         ),
         (
@@ -184,7 +176,7 @@
             me > 0,
         ),
     )
-    for copy, sends, _ in halos:
+    for copy, sends, _ in halos[:1] + halos[3:]:
 
         @pl.when(sends)
         def _(copy=copy):
@@ -289,7 +281,17 @@
     var = spread(member(channel_e, lane_e, GROUPS)) / cnt - mean * mean
     scale = rows_v[0] * (1.0 / jnp.sqrt(var + 1e-05))
 
-    for copy, _, receives in halos:
+    @pl.when(me > 0)
+    def _():
+        halos[0][0].wait_recv()
+
+    for copy, sends, _ in halos[1:3]:
+
+        @pl.when(sends)
+        def _(copy=copy):
+            copy.start()
+
+    for copy, _, receives in halos[1:]:
 
         @pl.when(receives)
         def _(copy=copy):
@@ -370,12 +372,19 @@
     slots = (shards - 1) * per_peer
     far = shards // 2 * per_peer
 
-    def target(i):
-        if per_peer <= 2:
-            inside = 1 - i // (slots // 2 * 2)
-            i = i + inside * lax.rem(row, 2) * (1 - 2 * lax.rem(i, 2))
-            i = i // 2 + (1 - lax.rem(i, 2)) * (far - 1)
-        return flipped(me, shards - 1 - i // per_peer, shards), lax.rem(i, per_peer)
+    rounds = far - direct
+    if far + 2 * rounds > slots:
+        rounds = 0
+
+    def target(u):
+        return flipped(me, shards - 1 - u // per_peer, shards), lax.rem(u, per_peer)
+
+    def mixed(i):
+        odd = lax.rem(row, 2)
+        g, h = i // 3, lax.rem(i, 3)
+        is_far = (1 - odd) * ((2 - h) // 2) + odd * lax.rem(h, 2)
+        near = far + 2 * g + (1 - odd) * (h - 1) + odd * (h // 2)
+        return is_far * (direct + g) + (1 - is_far) * near
 
     @pl.loop(0, direct)
     def _(i):
@@ -399,11 +408,18 @@
 
         convolve(g * group)
 
-    @pl.loop(direct, (shards - 1) * per_peer)
-    def _(i):
-        d, q = target(i)
+    def send(u):
+        d, q = target(u)
         slot_frame(d * per_peer + q, lambda t, k: t + BACK - k)
         exchange(d, me, q).start()
+
+    @pl.loop(0, slots - direct)
+    def _(i):
+        if rounds:
+            inside = 1 - i // (3 * rounds)
+            send(inside * mixed(inside * i) + (1 - inside) * (direct + i))
+        else:
+            send(direct + i)
 
     def keep(q):
         return pltpu.make_async_copy(

time: 133 us -> 140 us (1.053)
  Pallas kernels: 132 us -> 138 us
    pallas_call x1, Pallas kernels: 124 us -> 131 us  [body(): pl.pallas_call(functools.partial(block_kernel, shards, bands, width), out...]
where the time goes in v4:
time: 140 us
  Pallas kernels  138 us (99%)
  other arithmetic  1.42 us (1%)
    pallas_call x1, Pallas kernels, body(): pl.pallas_call(functools.partial(block_kernel, shards, bands, width), out...  131 us
    pallas_call x1, Pallas kernels, body(): pl.pallas_call(lift_kernel, out_shape=jax.ShapeDtypeStruct((count, cells,...  7.67 us

profile of v4, /device:TPU:0, one launch (start us, length us, event | category | flops | bytes accessed | tf_op | source)
XLA Modules:
  0.0 139.8 jit_solution(7129144466320750620)
XLA Ops:
  0.0 0.7 and_select_fusion.1
  0.7 0.1 convert_reduce_fusion
  0.8 0.7 select_reduce_fusion
  1.4 130.7 %block.1 = (bf16[16,512,256]{2,1,0:T(8,128)(2,1)}, s32[8,1,128]{2,1,0:T(1,128)}) custom-call(s32[16]{0:T(128)} %get-tuple-element.10.order_ref, s32[16]{0:T(128)} %get-tuple-element.9.position_ref, s32[16]{0:T(128)} %clip_ref.1, bf16[16,512,256]{2,1,0:T(8,128)(2,1)} %bitcast.7, f32[1,256]{1,0:T(1,128)} %bitcast.9, f32[1,256]{1,0:T(1,128)} %bitcast.10, ...), custom_call_target="tpu_custom_call" | custom-call | tf_op jit(solution)/shard_map/block/pallas_call | solution.py:524
  132.1 7.7 %lift.1 = bf16[16,512,512]{2,1,0:T(8,128)(2,1)} custom-call(s32[8,1,128]{2,1,0:T(1,128)} %get-tuple-element.7.pos_ref, bf16[16,512,256]{2,1,0:T(8,128)(2,1)} %get-tuple-element.8.x_hbm, bf16[256,512]{1,0:T(8,128)(2,1)} %w_hbm.1), custom_call_target="tpu_custom_call" | custom-call | tf_op jit(solution)/shard_map/lift/pallas_call | solution.py:576
  (1 shorter events, 0.0 us)
